TPU v7x, 512 devices: a whole 4x4x16 slice. The times are simulated.
512 devices in a mesh: dp: 32 (over z_hi, y, core), tensor: 16 (over x, z_lo).
Axes of the slice: x: 4, y: 4, z: 16 (z_hi: 4, z_lo: 4; z = z_hi * 4 + z_lo), core: 2. Of those that a mesh axis runs over, the one named last changes fastest.
Arguments:
- gate_in: bfloat16 [4096, 14336], P('dp', 'tensor'), may hold values from -8 to 8
- up_in: bfloat16 [4096, 14336], P('dp', 'tensor'), may hold values from -6 to 6
- cotangent: bfloat16 [4096, 4096], P(('dp', 'tensor')), may hold values from -6 to 6
- w_down: bfloat16 [16, 128, 128, 128], P('tensor', 'dp'), may hold values from -0.125 to 0.125
- block_hidden: int32 [16, 128], P('tensor'), may hold values from 0 to 6, as said below
- block_feat: int32 [16, 128], P('tensor'), may hold values from 0 to 31, as said below
- kept_counts: int32 [16], P('tensor'), may hold values from 64 to 128, as said below
Outputs:
- grad_gate: bfloat16 [4096, 14336], P('dp', 'tensor')
- grad_up: bfloat16 [4096, 14336], P('dp', 'tensor')
- grad_down: bfloat16 [16, 128, 128, 128], P('tensor', 'dp')
Inputs may be any that keep to these rules, and one draw needn't show every extreme that they name: `block_hidden`: within one shard the 128 slots name distinct pairs of hidden block and feature block; slots past the shard's count are filled with further distinct pairs. `block_feat`: same pairs as block_hidden. `kept_counts`: some shard keeps all 128 slots in every draw.
All inputs are finite; a program needn't handle non-finite values.
Results may differ from a plain program's by a relative error of at most 0.023.
Values may be sent and summed in bfloat16 or wider, within the bound.
A program may use at most 64 MiB of HBM per device.

v0:
```python
import math

import jax
import jax.numpy as jnp
from jax import lax
from jax.sharding import PartitionSpec as P


def per_device(gate_in, up_in, cotangent, w_down, block_hidden, block_feat, kept_counts):
    tokens = gate_in.shape[0]
    block = w_down.shape[2]
    hidden_blocks = gate_in.shape[1] // block
    total_slots = block_hidden.shape[1]
    gate_f = gate_in.astype(jnp.float32)
    up_f = up_in.astype(jnp.float32)
    sigma = jax.nn.sigmoid(gate_f)
    active = gate_f * sigma
    hidden = (active * up_f).astype(jnp.bfloat16).reshape(tokens, hidden_blocks, block)
    rows_all = lax.all_gather(cotangent, "tensor", axis=0, tiled=True)
    feature_parts = rows_all.reshape(tokens, -1, block)
    hidden_ids = block_hidden[0]
    feature_ids = block_feat[0]
    keep = (jnp.arange(total_slots, dtype=jnp.int32) < kept_counts[0]).astype(jnp.float32)
    empty = jnp.zeros((tokens, hidden_blocks, block), jnp.float32)
    every = lax.all_gather(w_down, "dp", axis=1, tiled=True)
    pieces = every[0]
    count = pieces.shape[0]
    slot_group = math.gcd(count, 16)

    def slot_one_group(step, accum):
        local = step * slot_group
        hid = lax.dynamic_slice_in_dim(hidden_ids, local, slot_group)
        feat = lax.dynamic_slice_in_dim(feature_ids, local, slot_group)
        live = lax.dynamic_slice_in_dim(keep, local, slot_group)
        weights = lax.dynamic_slice_in_dim(pieces, local, slot_group, 0)
        picked = jnp.take(feature_parts, feat, axis=1)
        contrib = jnp.einsum("tsf,shf->tsh", picked, weights, preferred_element_type=jnp.float32)
        for inner in range(slot_group):
            target = hid[inner]
            current = lax.dynamic_slice_in_dim(accum, target, 1, 1)
            added = current + contrib[:, inner : inner + 1, :] * live[inner]
            accum = lax.dynamic_update_slice_in_dim(accum, added, target, 1)
        return accum

    grad_parts = lax.fori_loop(0, count // slot_group, slot_one_group, empty)
    count = lax.axis_size("dp") * w_down.shape[1]
    group = math.gcd(count, 16)

    def grad_one_group(step, result):
        local = step * group
        hid = lax.dynamic_slice_in_dim(hidden_ids, local, group)
        feat = lax.dynamic_slice_in_dim(feature_ids, local, group)
        live = lax.dynamic_slice_in_dim(keep, local, group)
        chosen = jnp.take(hidden, hid, axis=1)
        picked = jnp.take(feature_parts, feat, axis=1)
        term = jnp.einsum("tsh,tsf->shf", chosen, picked, preferred_element_type=jnp.float32)
        return lax.dynamic_update_slice_in_dim(result, term * live[:, None, None], local, 0)

    shares = lax.psum_scatter(
        lax.fori_loop(
            0, count // group, grad_one_group, jnp.zeros((count, block, block), jnp.float32)
        ).astype(jnp.bfloat16),
        "dp",
        scatter_dimension=0,
        tiled=True,
    )
    grad_down = shares.reshape(w_down.shape)
    grad_hidden = grad_parts.reshape(tokens, hidden_blocks * block)
    grad_gate = (grad_hidden * up_f * sigma * (1.0 + gate_f * (1.0 - sigma))).astype(jnp.bfloat16)
    grad_up = (grad_hidden * active).astype(jnp.bfloat16)
    return (grad_gate, grad_up, grad_down)


def solution(mesh):
    return jax.shard_map(
        per_device,
        mesh=mesh,
        in_specs=(
            P("dp", "tensor"),
            P("dp", "tensor"),
            P(("dp", "tensor"), None),
            P("tensor", "dp", None, None),
            P("tensor", None),
            P("tensor", None),
            P("tensor"),
        ),
        out_specs=(P("dp", "tensor"), P("dp", "tensor"), P("tensor", "dp", None, None)),
        check_vma=False,
    )
```

profile of v0, /device:TPU:1, one launch (start us, length us, event | category | flops | bytes accessed | tf_op | source)
XLA Modules:
  0.0 726.8 jit_solution(15751729633838718528)
XLA Ops:
  9.4 1.1 copy.34
  10.5 1.1 copy.33
  11.6 81.7 %all-gather.5.cloned.1.call-done = bf16[128,4096]{1,0:T(8,128)(2,1)} async-done(((bf16[8,4096]{1,0:T(8,128)(2,1)}), bf16[128,4096]{1,0:T(8,128)(2,1)}) %all-gather.5.cloned.1.call-update) | async-done | bytes 1048592 | tf_op jit(solution)/shard_map/all_gather | solution.py:19
  93.3 1.6 copy.31
  95.6 105.5 %all-gather.3.cloned.1.call-done = bf16[1,128,128,128]{3,2,0,1:T(8,128)(2,1)} async-done(((bf16[1,4,128,128]{3,2,0,1:T(8,128)(2,1)}), bf16[1,128,128,128]{3,2,0,1:T(8,128)(2,1)}) %all-gather.3.cloned.1.call-update) | async-done | bytes 4194320 | tf_op jit(solution)/shard_map/all_gather | solution.py:25
  201.2 361.6 %while.26 = (s32[]{:T(128)}, f32[128,7,128]{0,2,1:T(8,128)S(1)}, s32[128]{0:T(128)S(1)}, bf16[128,128,128]{2,1,0:T(8,128)(2,1)}, s32[128]{0:T(128)S(1)}, /*index...) while((s32[]{:T(128)}, f32[128,7,128]{0,2,1:T(8,128)S(1)}, ...), condition=%wide.region_1.3_spmd, body=%wide.region_0.2_spmd.sunk | while | flops 67896424 | bytes 6297203 | solution.py:45
  201.4 0.7 fusion.84
  232.8 0.7 fusion.85
  234.2 1.6 convolution_bitcast_fusion.2
  240.4 0.7 fusion.93
  246.6 0.7 fusion.84
  278.0 0.7 fusion.85
  279.4 1.6 convolution_bitcast_fusion.2
  285.6 0.7 fusion.93
  291.8 0.7 fusion.84
  323.2 0.7 fusion.85
  324.6 1.6 convolution_bitcast_fusion.2
  330.8 0.7 fusion.93
  337.0 0.7 fusion.84
  368.4 0.7 fusion.85
  369.8 1.6 convolution_bitcast_fusion.2
  382.2 0.7 fusion.84
  413.6 0.7 fusion.85
  415.0 1.6 convolution_bitcast_fusion.2
  421.1 0.7 fusion.93
  427.4 0.7 fusion.84
  458.8 0.7 fusion.85
  460.2 1.6 convolution_bitcast_fusion.2
  472.6 0.7 fusion.84
  504.0 0.7 fusion.85
  505.4 1.6 convolution_bitcast_fusion.2
  511.5 0.7 fusion.93
  517.8 0.7 fusion.84
  549.2 0.7 fusion.85
  550.6 1.6 convolution_bitcast_fusion.2
  563.2 3.0 broadcast_in_dim.43
  566.2 21.8 %while.27 = (s32[]{:T(128)}, bf16[128,128,128]{2,1,0:T(8,128)(2,1)}, s32[128]{0:T(128)S(1)}, bf16[128,7,128]{2,0,1:T(8,128)(2,1)S(1)}, s32[128]{0:T(128)S(1)}, /...) while((s32[]{:T(128)}, ...), condition=%wide.region_3.5_spmd, body=%wide.region_2.4_spmd.sunk | while | flops 67897544 | bytes 4203431 | solution.py:60
  567.7 1.2 fusion.104
  570.4 1.2 fusion.104
  573.1 1.3 fusion.104
  575.9 1.2 fusion.104
  578.6 1.2 fusion.104
  581.3 1.2 fusion.104
  584.1 1.2 fusion.104
  586.8 1.2 fusion.104
  588.1 0.8 copy.38
  588.9 0.8 copy.37
  589.7 130.6 %reduce-scatter.2.cloned.1.call-done = bf16[4,128,128]{2,1,0:T(8,128)(2,1)} async-done(((bf16[128,128,128]{2,1,0:T(8,128)(2,1)}), bf16[4,128,128]{2,1,0:T(8,128)(2,1)}) %reduce-scatter.2.cloned.1.call-update) | async-done | bytes 131088 | tf_op jit(solution)/shard_map/reduce_scatter | solution.py:59
  (226 shorter events, 101.3 us)
Async XLA Ops:
  7.2 194.0 %copy-start = (s32[1,128]{1,0:T(1,128)S(1)}, s32[1,128]{1,0:T(1,128)}, u32[]{:S(2)}) copy-start(s32[1,128]{1,0:T(1,128)} %param.18) | copy-start | bytes 1540
  7.2 194.0 %copy-start.1 = (s32[1,128]{1,0:T(1,128)S(1)}, s32[1,128]{1,0:T(1,128)}, u32[]{:S(2)}) copy-start(s32[1,128]{1,0:T(1,128)} %param.17) | copy-start | bytes 1540
  7.2 86.1 %all-gather.5.cloned.1.call-start = ((), (), s32[]{:S(2)}) async-start(), calls=%async_computation.2 | async-start | bytes 1114112 | tf_op jit(solution)/shard_map/all_gather | solution.py:19
  7.9 193.2 %all-gather.3.cloned.1.call-start = ((), (), s32[]{:S(2)}) async-start(), calls=%async_computation.1 | async-start | bytes 4325376 | tf_op jit(solution)/shard_map/all_gather | solution.py:25
  8.7 711.6 %reduce-scatter.2.cloned.1.call-start = ((), (), s32[]{:S(2)}) async-start(), calls=%async_computation.3 | async-start | bytes 4325376 | tf_op jit(solution)/shard_map/reduce_scatter | solution.py:59
Sparse Core Ops, SparseCore 0:
  10.1 83.1 all-gather.4
  96.4 104.6 all-gather.2
  588.2 132.0 reduce-scatter.1
where the time goes:
time: 732 us; the launch traced here: 727 us
  waiting for transfers between devices  319 us (44%)
  loops' own time  247 us (34%)
  other arithmetic  85.1 us (12%)
  local copies, waits for them, and re-layouts  38.3 us (5%)
  matrix products  22.7 us (3%)
  between operations  14.5 us (2%)
    another operation x1, loops' own time, per_device(): grad_parts = lax.fori_loop(0, count // slot_group, slot_one_group, empty)  247 us
    reduce_scatter x1, waiting for transfers between devices, per_device(): lax.psum_scatter(lax.fori_loop(0, count // group, grad_one_group, jnp.zer...  131 us
    all_gather x1, waiting for transfers between devices, per_device(): every = lax.all_gather(w_down, 'dp', axis=1, tiled=True)  106 us
    dynamic_update_slice x128, other arithmetic, slot_one_group(): accum = lax.dynamic_update_slice_in_dim(accum, added, target, 1)  83.4 us
    all_gather x1, waiting for transfers between devices, per_device(): rows_all = lax.all_gather(cotangent, 'tensor', axis=0, tiled=True)  81.7 us
  transfers between devices with their start and end apart: 3, of which 3 were waited for; matrix products, arithmetic and copies ran while one was open for 1% of the time, Pallas kernels for 0%

commit v1 on v0

v1 whole, which is shorter than its diff:
```python
import jax
import jax.numpy as jnp
from jax import lax
from jax.experimental import pallas as pl
from jax.experimental.pallas import tpu as pltpu
from jax.sharding import PartitionSpec as P

MESH = pl.DeviceIdType.MESH
F32 = jnp.float32
BF16 = jnp.bfloat16


def kernel(
    gate, up, cot, w, hid_ids, feat_ids, count,
    gg, gu, gd,
    raw, feats, hid_t, weights, spread, total, other,
    prod, s1, r1, s2, r2, part, t1, u1, t2, u2,
    send_sems, recv_sems,
):
    dp, tn = lax.axis_index("dp"), lax.axis_index("tensor")
    zh, y, c = dp // 8, (dp // 2) % 4, dp % 2
    x, zl = tn // 4, tn % 4

    def dev(dz=0, dy=0, other_core=False, dx=0, dl=0):
        core = 1 - c if other_core else c
        return (
            ((zh + dz) % 4) * 8 + ((y + dy) % 4) * 2 + core,
            ((x + dx) % 4) * 4 + (zl + dl) % 4,
        )

    sib = dev(other_core=True)
    yd = {1: dev(dy=1), -1: dev(dy=3)}
    zd = {1: dev(dz=1), -1: dev(dz=3)}
    xd = {1: dev(dx=1), -1: dev(dx=3)}
    ld = {k: dev(dl=k) for k in (1, 2, 3)}

    names = {}
    sent = []

    def number(name):
        return names.setdefault(name, len(names))

    def send(name, src, dst, to):
        i = number(name)
        copy = pltpu.make_async_remote_copy(
            src_ref=src, dst_ref=dst, send_sem=send_sems.at[i], recv_sem=recv_sems.at[i],
            device_id=to, device_id_type=MESH,
        )
        copy.start()
        sent.append(copy)

    def arrive(name, dst):
        i = number(name)
        pltpu.make_async_remote_copy(
            src_ref=dst, dst_ref=dst, send_sem=send_sems.at[i], recv_sem=recv_sems.at[i],
            device_id=sib, device_id_type=MESH,
        ).wait_recv()

    barrier = pltpu.get_barrier_semaphore()
    partners = [sib, *yd.values(), *zd.values(), *xd.values(), *ld.values()]
    for partner in partners:
        pl.semaphore_signal(barrier, inc=1, device_id=partner, device_id_type=MESH)

    weights[zh * 4 + y] = w[0]
    for fp in range(16):
        low = cot[:, fp * 128 : (fp + 1) * 128].astype(F32)
        high = cot[:, (fp + 16) * 128 : (fp + 17) * 128].astype(F32)
        raw[c, tn, fp] = jnp.concatenate([low, high], axis=0).astype(BF16)

    pl.semaphore_wait(barrier, len(partners))

    def cot_block(dx, k):
        return raw.at[c, ((x + dx) % 4) * 4 + (zl - k + 4) % 4]

    def cot_half(dx, k, half):
        return raw.at[c, ((x + dx) % 4) * 4 + (zl - k + 4) % 4, pl.ds(half * 8, 8)]

    def cot_sib(dx, k):
        return raw.at[1 - c, ((x + dx) % 4) * 4 + (zl - k + 4) % 4]

    def w_half(dz, dy, half):
        return weights.at[((zh + dz) % 4) * 4 + (y + dy) % 4, pl.ds(half * 2, 2)]

    def cot_out(k):
        own = cot_block(0, k)
        send(("ax", 1, k), own, own, xd[1])
        send(("ax", -1, k), own, own, xd[-1])
        send(("as", 0, k), own, own, sib)

    def w_out(dz, order=((1, 0), (-1, 1), (1, 1), (-1, 0))):
        for way, half in order:
            block = w_half(dz, 0, half)
            send(("by", way, dz, half), block, block, yd[way])

    def w_out_half(dz, half):
        block = w_half(dz, 0, half)
        for way in (1, -1):
            send(("by", way, dz, half), block, block, yd[way])

    def w_in(way, dz, half):
        block = w_half(dz, -way % 4, half)
        arrive(("by", way, dz, half), block)
        if (way, half) in ((1, 0), (-1, 1)):
            send(("bf", way, dz), block, block, yd[way])

    def w_in_forwards(dz):
        w_in(1, dz, 0)
        w_in(-1, dz, 1)

    def w_in_rest(dz):
        w_in(1, dz, 1)
        w_in(-1, dz, 0)
        arrive(("bf", 1, dz), w_half(dz, 2, 0))
        arrive(("bf", -1, dz), w_half(dz, 2, 1))

    own = cot_block(0, 0)
    for k in (1, 2, 3):
        send(("al", k), own, own, ld[k])
    cot_out(0)
    for way, half in ((1, 0), (-1, 1), (1, 1), (-1, 0)):
        block = w_half(0, 0, half)
        send(("bz", way, half), block, block, zd[way])
    w_out(0)

    for j in range(7):
        cols = slice(j * 128, (j + 1) * 128)
        g = gate[:, cols].astype(F32)
        active = g * (1.0 / (1.0 + jnp.exp(-g)))
        hidden = (active * up[:, cols].astype(F32)).astype(BF16)
        hid_t[c, j] = hidden.astype(F32).T.astype(BF16)
    send("hid", hid_t.at[c], hid_t.at[c], sib)

    def cot_in_lo(k):
        arrive(("al", k), cot_block(0, k))
        cot_out(k)

    def cot_in_x(k):
        for way, half in ((1, 0), (-1, 1)):
            arrive(("ax", way, k), cot_block(-way, k))
            piece = cot_half(-way, k, half)
            send(("af", way, k), piece, piece, xd[way])
            block = cot_block(-way, k)
            send(("as", -way, k), block, block, sib)

    def cot_in_far(k):
        arrive(("af", 1, k), cot_half(2, k, 0))
        arrive(("af", -1, k), cot_half(2, k, 1))
        block = cot_block(2, k)
        send(("as", 2, k), block, block, sib)

    def wz_in(way, half):
        block = w_half(-way, 0, half)
        arrive(("bz", way, half), block)
        if (way, half) in ((1, 0), (-1, 1)):
            send(("bzf", way), block, block, zd[way])
        w_out_half(-way, half)

    for k in (1, 2, 3):
        cot_in_lo(k)
    cot_in_x(0)
    w_in_forwards(0)
    cot_in_x(1)
    cot_in_x(2)
    cot_in_far(0)
    cot_in_x(3)
    wz_in(1, 0)
    wz_in(-1, 1)
    cot_in_far(1)
    cot_in_far(2)
    cot_in_far(3)

    for k in range(4):
        for dx in (0, 1, -1, 2):
            arrive(("as", dx, k), cot_sib(dx, k))
    arrive("hid", hid_t.at[1 - c])

    def repack(i, carry):
        core, pair = i // 8, i % 8
        first = raw[core, 2 * pair].astype(F32)
        second = raw[core, 2 * pair + 1].astype(F32)
        feats[0:16, i] = jnp.concatenate([first[:, :8], second[:, :8]], axis=1).astype(BF16)
        feats[16:32, i] = jnp.concatenate([first[:, 8:], second[:, 8:]], axis=1).astype(BF16)
        return carry

    lax.fori_loop(0, 16, repack, 0)

    def products(dz):
        def place(dy, carry):
            base = ((((zh + dz) % 4) * 4 + (y + dy) % 4) * 2 + c) * 4
            for q in range(4):
                hid = hid_ids[0, base + q]
                feat = feat_ids[0, base + q]
                left = jnp.concatenate([hid_t[0, hid], hid_t[1, hid]], axis=1)
                right = feats[feat].reshape(256, 128)
                prod[dz, dy, q] = jnp.dot(left, right, preferred_element_type=F32)
            return carry

        lax.fori_loop(0, 4, place, 0)

    def c1(dz):
        products(dz)
        for half, way in ((0, 1), (1, -1)):
            s1[dz, half] = prod[dz, 2, 2 * half : 2 * half + 2].astype(BF16)
            send(("c1", dz, half), s1.at[dz, half], r1.at[dz, half], yd[way])

    def c2(dz):
        for half, way, dy in ((0, 1, 1), (1, -1, 3)):
            rest = 1 - half
            s2[dz, half, 2 * rest : 2 * rest + 2] = prod[dz, dy, 2 * rest : 2 * rest + 2].astype(BF16)
            arrive(("c1", dz, half), r1.at[dz, half])
            s2[dz, half, 2 * half : 2 * half + 2] = (
                prod[dz, dy, 2 * half : 2 * half + 2] + r1[dz, half].astype(F32)
            ).astype(BF16)
            send(("c2", dz, half), s2.at[dz, half], r2.at[dz, half], yd[way])

    def c3(dz):
        arrive(("c2", dz, 0), r2.at[dz, 0])
        arrive(("c2", dz, 1), r2.at[dz, 1])
        part[dz] = prod[dz, 0] + r2[dz, 0].astype(F32) + r2[dz, 1].astype(F32)

    def d1():
        for half, way in ((0, 1), (1, -1)):
            t1[half] = part[2, 2 * half : 2 * half + 2].astype(BF16)
            send(("d1", half), t1.at[half], u1.at[half], zd[way])

    def d2():
        for half, way, dz in ((0, 1, 1), (1, -1, 3)):
            rest = 1 - half
            t2[half, 2 * rest : 2 * rest + 2] = part[dz, 2 * rest : 2 * rest + 2].astype(BF16)
            arrive(("d1", half), u1.at[half])
            t2[half, 2 * half : 2 * half + 2] = (
                part[dz, 2 * half : 2 * half + 2] + u1[half].astype(F32)
            ).astype(BF16)
            send(("d2", half), t2.at[half], u2.at[half], zd[way])

    c1(2)
    wz_in(1, 1)
    wz_in(-1, 0)
    c1(1)
    c2(2)
    c1(3)
    c2(1)
    c3(2)
    d1()
    c1(0)
    c2(3)
    c3(1)
    w_in_rest(0)
    w_in_forwards(1)
    w_in_forwards(-1)
    c2(0)
    c3(3)
    d2()
    c3(0)
    for way, half in ((1, 0), (-1, 1)):
        arrive(("bzf", way), w_half(2, 0, half))
        w_out_half(2, half)
    w_in_rest(1)
    w_in_rest(-1)
    w_in_forwards(2)
    w_in_rest(2)

    kept = count[0]
    total[...] = jnp.zeros_like(total)

    def accumulate(i, carry):
        base = (i * 2 + c) * 4
        picked = []
        for q in range(4):
            hid = jnp.where(base + q < kept, hid_ids[0, base + q], -1)
            picked.append(feats[feat_ids[0, base + q]].reshape(256, 128))
            block = weights[i, q]
            for j in range(7):
                spread[j * 128 : (j + 1) * 128, q * 128 : (q + 1) * 128] = jnp.where(
                    hid == j, block, jnp.zeros_like(block)
                )
        total[...] += lax.dot_general(
            jnp.concatenate(picked, axis=1), spread[...], (((1,), (1,)), ((), ())),
            preferred_element_type=F32,
        )
        return carry

    lax.fori_loop(0, 16, accumulate, 0)

    send("gh", total.at[pl.ds(pl.multiple_of((1 - c) * 128, 128), 128)], other, sib)

    arrive(("d2", 0), u2.at[0])
    arrive(("d2", 1), u2.at[1])
    for q in range(4):
        mine = part[0, q] + u2[0, q].astype(F32) + u2[1, q].astype(F32)
        live = jnp.where(dp * 4 + q < kept, 1.0, 0.0)
        gd[0, q] = (mine * live).astype(BF16)

    arrive("gh", other)
    for j in range(7):
        cols = slice(j * 128, (j + 1) * 128)
        grad = total[pl.ds(pl.multiple_of(c * 128, 128), 128), cols] + other[:, cols]
        g = gate[:, cols].astype(F32)
        u = up[:, cols].astype(F32)
        sigma = 1.0 / (1.0 + jnp.exp(-g))
        gg[:, cols] = (grad * u * sigma * (1.0 + g * (1.0 - sigma))).astype(BF16)
        gu[:, cols] = (grad * (g * sigma)).astype(BF16)

    for copy in sent:
        copy.wait_send()
    assert len(names) <= send_sems.shape[0]


def per_device(gate_in, up_in, cotangent, w_down, block_hidden, block_feat, kept_counts):
    vmem = pl.BlockSpec(memory_space=pltpu.VMEM)
    smem = pl.BlockSpec(memory_space=pltpu.SMEM)
    copies = 112
    return pl.pallas_call(
        kernel,
        out_shape=(
            jax.ShapeDtypeStruct(gate_in.shape, BF16),
            jax.ShapeDtypeStruct(up_in.shape, BF16),
            jax.ShapeDtypeStruct(w_down.shape, BF16),
        ),
        in_specs=[vmem, vmem, vmem, vmem, smem, smem, smem],
        out_specs=(vmem, vmem, vmem),
        scratch_shapes=[
            pltpu.VMEM((2, 16, 16, 16, 128), BF16),
            pltpu.VMEM((32, 16, 16, 128), BF16),
            pltpu.VMEM((2, 7, 128, 128), BF16),
            pltpu.VMEM((16, 4, 128, 128), BF16),
            pltpu.VMEM((896, 512), BF16),
            pltpu.VMEM((256, 896), F32),
            pltpu.VMEM((128, 896), F32),
            pltpu.VMEM((4, 4, 4, 128, 128), F32),
            pltpu.VMEM((4, 2, 2, 128, 128), BF16),
            pltpu.VMEM((4, 2, 2, 128, 128), BF16),
            pltpu.VMEM((4, 2, 4, 128, 128), BF16),
            pltpu.VMEM((4, 2, 4, 128, 128), BF16),
            pltpu.VMEM((4, 4, 128, 128), F32),
            pltpu.VMEM((2, 2, 128, 128), BF16),
            pltpu.VMEM((2, 2, 128, 128), BF16),
            pltpu.VMEM((2, 4, 128, 128), BF16),
            pltpu.VMEM((2, 4, 128, 128), BF16),
            pltpu.SemaphoreType.DMA((copies,)),
            pltpu.SemaphoreType.DMA((copies,)),
        ],
        compiler_params=pltpu.CompilerParams(
            collective_id=0, has_side_effects=True, vmem_limit_bytes=48 * 2**20
        ),
    )(gate_in, up_in, cotangent, w_down, block_hidden, block_feat, kept_counts)


def solution(mesh):
    return jax.shard_map(
        per_device,
        mesh=mesh,
        in_specs=(
            P("dp", "tensor"),
            P("dp", "tensor"),
            P(("dp", "tensor"), None),
            P("tensor", "dp", None, None),
            P("tensor", None),
            P("tensor", None),
            P("tensor"),
        ),
        out_specs=(P("dp", "tensor"), P("dp", "tensor"), P("tensor", "dp", None, None)),
        check_vma=False,
    )
```

time: 732 us -> 92.5 us (0.13)
  waiting for transfers between devices: 319 us -> 0 us
  loops' own time: 247 us -> 0 us
  other arithmetic: 85.1 us -> 0 us
  Pallas kernels: 0 us -> 84.5 us
  local copies, waits for them, and re-layouts: 38.3 us -> 5.65 us
  matrix products: 22.7 us -> 0 us
  between operations: 14.5 us -> 1.35 us
    another operation x2 -> x0, loops' own time: 247 us -> none  [the longest x1 247 us: per_device(): grad_parts = lax.fori_loop(0, count // slot_group, slot_one_group, empty)]
    all_gather x2 -> x0, waiting for transfers between devices: 187 us -> none  [the longest x1 106 us: per_device(): every = lax.all_gather(w_down, 'dp', axis=1, tiled=True)]
    reduce_scatter x1 -> x0, waiting for transfers between devices: 131 us -> none  [per_device(): lax.psum_scatter(lax.fori_loop(0, count // group, grad_one_group, jnp.zer...]
    pallas_call x0 -> x1, Pallas kernels: none -> 84.5 us  [per_device(): pl.pallas_call(kernel, out_shape=(jax.ShapeDtypeStruct(gate_in.shape, BF1...]
    dynamic_update_slice x128 -> x0, other arithmetic: 83.4 us -> none  [slot_one_group(): accum = lax.dynamic_update_slice_in_dim(accum, added, target, 1)]
    dot_general x16 -> x0, matrix products: 22.7 us -> none  [the longest x8 12.8 us: slot_one_group(): jnp.einsum('tsf,shf->tsh', picked, weights, preferred_element_type=jnp.fl...]
    gather x24 -> x0, local copies, waits for them, and re-layouts: 15.5 us -> none  [the longest x8 5.18 us: grad_one_group(): chosen = jnp.take(hidden, hid, axis=1)]
    slice x16 -> x0, local copies, waits for them, and re-layouts: 11.6 us -> none  [the longest x8 5.78 us: slot_one_group(): added = current + contrib[:, inner:inner + 1, :] * live[inner]]
  transfers between devices with their start and end apart: 3 -> 0, of which waited for: 3 -> 0; matrix products, arithmetic and copies ran while one was open for 1% -> 0% of each run, Pallas kernels for 0% -> 0%
where the time goes in v1:
time: 92.5 us; the launch traced here: 91.5 us
  Pallas kernels  84.5 us (91%)
  local copies, waits for them, and re-layouts  5.65 us (6%)
  between operations  1.35 us (1%)
    pallas_call x1, Pallas kernels, per_device(): pl.pallas_call(kernel, out_shape=(jax.ShapeDtypeStruct(gate_in.shape, BF1...  84.5 us
    unnamed x15, local copies, waits for them, and re-layouts  5.65 us

profile of v1, /device:TPU:1, one launch (start us, length us, event | category | flops | bytes accessed | tf_op | source)
XLA Modules:
  0.0 91.5 jit_solution(13986593027804710542)
XLA Ops:
  0.6 0.0 copy-start.5
  0.6 0.0 copy-start.4
  1.3 0.0 copy-done.5
  1.3 0.0 copy-done.4
  1.3 0.0 copy-start
  1.3 0.9 %copy-done = bf16[128,896]{1,0:T(8,128)(2,1)S(1)} copy-done((bf16[128,896]{1,0:T(8,128)(2,1)S(1)}, bf16[128,896]{1,0:T(8,128)(2,1)}, u32[]{:S(2)}) %copy-start) | copy-done | bytes 229400
  2.3 0.0 copy-start.1
  2.3 0.9 %copy-done.1 = bf16[128,896]{1,0:T(8,128)(2,1)S(1)} copy-done((bf16[128,896]{1,0:T(8,128)(2,1)S(1)}, bf16[128,896]{1,0:T(8,128)(2,1)}, u32[]{:S(2)}) %copy-start.1) | copy-done | bytes 229400
  3.2 0.0 copy-start.2
  3.2 0.9 copy-done.2
  4.1 0.0 copy-start.3
  4.1 0.8 copy-done.3
  5.0 84.5 %shard_map.94 = (bf16[128,896]{1,0:T(8,128)(2,1)S(1)}, bf16[128,896]{1,0:T(8,128)(2,1)S(1)}, bf16[1,4,128,128]{3,2,1,0:T(8,128)(2,1)S(1)}) custom-call(bf16[128,896]{1,0:T(8,128)(2,1)S(1)} %copy-done, bf16[128,896]{1,0:T(8,128)(2,1)S(1)} %copy-done.1, bf16[8,4096]{1,0:T(8,128)(2,1)S(1)} %copy-done.3, bf16[1,4,128,128]{3,2,1,0:T(8,128)(2,1)S(1)} %copy-done.2, ...), custom_call_target="tpu_custom_call" | custom-call | tf_op jit(solution)/shard_map/pallas_call | solution.py:313
  89.4 0.7 copy.14
  90.1 0.7 copy.15
  90.8 0.7 copy.16
Async XLA Ops:
  0.6 0.7 copy-start.5
  0.6 0.7 copy-start.4
  1.3 0.9 %copy-start = (bf16[128,896]{1,0:T(8,128)(2,1)S(1)}, bf16[128,896]{1,0:T(8,128)(2,1)}, u32[]{:S(2)}) copy-start(bf16[128,896]{1,0:T(8,128)(2,1)} %gate.1) | copy-start | bytes 688132
  2.3 0.9 %copy-start.1 = (bf16[128,896]{1,0:T(8,128)(2,1)S(1)}, bf16[128,896]{1,0:T(8,128)(2,1)}, u32[]{:S(2)}) copy-start(bf16[128,896]{1,0:T(8,128)(2,1)} %up.1) | copy-start | bytes 688132
  3.2 0.9 copy-start.2
  4.1 0.8 copy-start.3

commit v2 on v1

--- a/solution.py
+++ b/solution.py
@@ -11,11 +11,11 @@
 
 
 def kernel(
-    gate, up, cot, w, hid_ids, feat_ids, count,
+    gate_hbm, up_hbm, cot_hbm, w_hbm, hid_ids, feat_ids, count,
     gg, gu, gd,
-    raw, feats, hid_t, weights, spread, total, other,
+    gate, up, cot, raw, feats, hid_t, weights, spread, total, other,
     prod, s1, r1, s2, r2, part, t1, u1, t2, u2,
-    send_sems, recv_sems,
+    send_sems, recv_sems, load_sems,
 ):
     dp, tn = lax.axis_index("dp"), lax.axis_index("tensor")
     zh, y, c = dp // 8, (dp // 2) % 4, dp % 2
@@ -35,7 +35,7 @@
     ld = {k: dev(dl=k) for k in (1, 2, 3)}
 
     names = {}
-    sent = []
+    sent, started, arrived = [], [], []
 
     def number(name):
         return names.setdefault(name, len(names))
@@ -48,9 +48,12 @@
         )
         copy.start()
         sent.append(copy)
+        started.append(name)
 
     def arrive(name, dst):
         i = number(name)
+        assert name in started, name
+        arrived.append(name)
         pltpu.make_async_remote_copy(
             src_ref=dst, dst_ref=dst, send_sem=send_sems.at[i], recv_sem=recv_sems.at[i],
             device_id=sib, device_id_type=MESH,
@@ -61,11 +64,31 @@
     for partner in partners:
         pl.semaphore_signal(barrier, inc=1, device_id=partner, device_id_type=MESH)
 
-    weights[zh * 4 + y] = w[0]
+    loads = [
+        pltpu.make_async_copy(src, dst, load_sems.at[n])
+        for n, (src, dst) in enumerate(
+            ((cot_hbm, cot), (gate_hbm, gate), (up_hbm, up), (w_hbm.at[0], weights.at[zh * 4 + y]))
+        )
+    ]
+    for load in loads:
+        load.start()
+
+    loads[0].wait()
     for fp in range(16):
         low = cot[:, fp * 128 : (fp + 1) * 128].astype(F32)
         high = cot[:, (fp + 16) * 128 : (fp + 17) * 128].astype(F32)
         raw[c, tn, fp] = jnp.concatenate([low, high], axis=0).astype(BF16)
+
+    loads[1].wait()
+    loads[2].wait()
+    for j in range(7):
+        cols = slice(j * 128, (j + 1) * 128)
+        g = gate[:, cols].astype(F32)
+        active = g * (1.0 / (1.0 + jnp.exp(-g)))
+        hidden = (active * up[:, cols].astype(F32)).astype(BF16)
+        hid_t[c, j] = hidden.astype(F32).T.astype(BF16)
+    total[...] = jnp.zeros_like(total)
+    loads[3].wait()
 
     pl.semaphore_wait(barrier, len(partners))
 
@@ -122,12 +145,6 @@
         send(("bz", way, half), block, block, zd[way])
     w_out(0)
 
-    for j in range(7):
-        cols = slice(j * 128, (j + 1) * 128)
-        g = gate[:, cols].astype(F32)
-        active = g * (1.0 / (1.0 + jnp.exp(-g)))
-        hidden = (active * up[:, cols].astype(F32)).astype(BF16)
-        hid_t[c, j] = hidden.astype(F32).T.astype(BF16)
     send("hid", hid_t.at[c], hid_t.at[c], sib)
 
     def cot_in_lo(k):
@@ -155,34 +172,21 @@
             send(("bzf", way), block, block, zd[way])
         w_out_half(-way, half)
 
-    for k in (1, 2, 3):
-        cot_in_lo(k)
-    cot_in_x(0)
-    w_in_forwards(0)
-    cot_in_x(1)
-    cot_in_x(2)
-    cot_in_far(0)
-    cot_in_x(3)
-    wz_in(1, 0)
-    wz_in(-1, 1)
-    cot_in_far(1)
-    cot_in_far(2)
-    cot_in_far(3)
-
-    for k in range(4):
-        for dx in (0, 1, -1, 2):
+    def repack(dx):
+        def step(i, carry):
+            core, pair = i // 2, ((x + dx) % 4) * 2 + i % 2
+            first = raw[core, 2 * pair].astype(F32)
+            second = raw[core, 2 * pair + 1].astype(F32)
+            at = core * 8 + pair
+            feats[0:16, at] = jnp.concatenate([first[:, :8], second[:, :8]], axis=1).astype(BF16)
+            feats[16:32, at] = jnp.concatenate([first[:, 8:], second[:, 8:]], axis=1).astype(BF16)
+            return carry
+
+        lax.fori_loop(0, 4, step, 0)
+
+    def from_sib(dx, ks):
+        for k in ks:
             arrive(("as", dx, k), cot_sib(dx, k))
-    arrive("hid", hid_t.at[1 - c])
-
-    def repack(i, carry):
-        core, pair = i // 8, i % 8
-        first = raw[core, 2 * pair].astype(F32)
-        second = raw[core, 2 * pair + 1].astype(F32)
-        feats[0:16, i] = jnp.concatenate([first[:, :8], second[:, :8]], axis=1).astype(BF16)
-        feats[16:32, i] = jnp.concatenate([first[:, 8:], second[:, 8:]], axis=1).astype(BF16)
-        return carry
-
-    lax.fori_loop(0, 16, repack, 0)
 
     def products(dz):
         def place(dy, carry):
@@ -197,95 +201,140 @@
 
         lax.fori_loop(0, 4, place, 0)
 
+    def pair(half):
+        return slice(2 * half, 2 * half + 2)
+
+    def piece(half):
+        return pl.ds(2 * half, 2)
+
     def c1(dz):
-        products(dz)
         for half, way in ((0, 1), (1, -1)):
-            s1[dz, half] = prod[dz, 2, 2 * half : 2 * half + 2].astype(BF16)
+            s1[dz, half] = prod[dz, 2, pair(half)].astype(BF16)
             send(("c1", dz, half), s1.at[dz, half], r1.at[dz, half], yd[way])
+        for half, way, dy in ((0, 1, 1), (1, -1, 3)):
+            rest = 1 - half
+            s2[dz, half, pair(rest)] = prod[dz, dy, pair(rest)].astype(BF16)
+            send(("cp", dz, half), s2.at[dz, half, piece(rest)], r2.at[dz, half, piece(rest)], yd[way])
 
     def c2(dz):
         for half, way, dy in ((0, 1, 1), (1, -1, 3)):
-            rest = 1 - half
-            s2[dz, half, 2 * rest : 2 * rest + 2] = prod[dz, dy, 2 * rest : 2 * rest + 2].astype(BF16)
             arrive(("c1", dz, half), r1.at[dz, half])
-            s2[dz, half, 2 * half : 2 * half + 2] = (
-                prod[dz, dy, 2 * half : 2 * half + 2] + r1[dz, half].astype(F32)
+            s2[dz, half, pair(half)] = (
+                prod[dz, dy, pair(half)] + r1[dz, half].astype(F32)
             ).astype(BF16)
-            send(("c2", dz, half), s2.at[dz, half], r2.at[dz, half], yd[way])
+            send(("cs", dz, half), s2.at[dz, half, piece(half)], r2.at[dz, half, piece(half)], yd[way])
 
     def c3(dz):
-        arrive(("c2", dz, 0), r2.at[dz, 0])
-        arrive(("c2", dz, 1), r2.at[dz, 1])
+        for half in (0, 1):
+            arrive(("cp", dz, half), r2.at[dz, half, piece(1 - half)])
+        for half in (0, 1):
+            arrive(("cs", dz, half), r2.at[dz, half, piece(half)])
         part[dz] = prod[dz, 0] + r2[dz, 0].astype(F32) + r2[dz, 1].astype(F32)
 
     def d1():
         for half, way in ((0, 1), (1, -1)):
-            t1[half] = part[2, 2 * half : 2 * half + 2].astype(BF16)
+            t1[half] = part[2, pair(half)].astype(BF16)
             send(("d1", half), t1.at[half], u1.at[half], zd[way])
+
+    def d2_plain(half, way, dz):
+        rest = 1 - half
+        t2[half, pair(rest)] = part[dz, pair(rest)].astype(BF16)
+        send(("dp", half), t2.at[half, piece(rest)], u2.at[half, piece(rest)], zd[way])
 
     def d2():
         for half, way, dz in ((0, 1, 1), (1, -1, 3)):
-            rest = 1 - half
-            t2[half, 2 * rest : 2 * rest + 2] = part[dz, 2 * rest : 2 * rest + 2].astype(BF16)
             arrive(("d1", half), u1.at[half])
-            t2[half, 2 * half : 2 * half + 2] = (
-                part[dz, 2 * half : 2 * half + 2] + u1[half].astype(F32)
-            ).astype(BF16)
-            send(("d2", half), t2.at[half], u2.at[half], zd[way])
-
+            t2[half, pair(half)] = (part[dz, pair(half)] + u1[half].astype(F32)).astype(BF16)
+            send(("ds", half), t2.at[half, piece(half)], u2.at[half, piece(half)], zd[way])
+
+    kept = count[0]
+
+    def accumulate(dz):
+        def place(dy, carry):
+            at = ((zh + dz) % 4) * 4 + (y + dy) % 4
+            base = (at * 2 + c) * 4
+            picked = []
+            for q in range(4):
+                hid = jnp.where(base + q < kept, hid_ids[0, base + q], -1)
+                picked.append(feats[feat_ids[0, base + q]].reshape(256, 128))
+                block = weights[at, q]
+                for j in range(7):
+                    spread[j * 128 : (j + 1) * 128, q * 128 : (q + 1) * 128] = jnp.where(
+                        hid == j, block, jnp.zeros_like(block)
+                    )
+            total[...] += lax.dot_general(
+                jnp.concatenate(picked, axis=1), spread[...], (((1,), (1,)), ((), ())),
+                preferred_element_type=F32,
+            )
+            return carry
+
+        lax.fori_loop(0, 4, place, 0)
+
+    cot_in_lo(1)
+    cot_in_lo(3)
+    cot_in_x(1)
+    cot_in_lo(2)
+    cot_in_x(0)
+    cot_in_x(3)
+    cot_in_x(2)
+    arrive("hid", hid_t.at[1 - c])
+    w_in_forwards(0)
+    from_sib(-1, (0, 1, 2, 3))
+    repack(3)
+    wz_in(1, 0)
+    wz_in(-1, 1)
+    from_sib(0, (0, 1, 2, 3))
+    repack(0)
+    cot_in_far(1)
+    cot_in_far(3)
+    cot_in_far(2)
+    cot_in_far(0)
+    from_sib(2, (0, 1, 2, 3))
+    repack(2)
+    from_sib(1, (0, 1, 2, 3))
+    repack(1)
+    w_in_rest(0)
+    products(2)
     c1(2)
+    products(1)
+    c1(1)
+    products(0)
+    c2(2)
+    products(3)
+    c1(3)
+    c3(2)
+    d1()
+    c2(1)
+    c2(3)
     wz_in(1, 1)
     wz_in(-1, 0)
-    c1(1)
-    c2(2)
-    c1(3)
-    c2(1)
-    c3(2)
-    d1()
-    c1(0)
-    c2(3)
+    accumulate(0)
+    c3(3)
     c3(1)
-    w_in_rest(0)
-    w_in_forwards(1)
-    w_in_forwards(-1)
-    c2(0)
-    c3(3)
-    d2()
-    c3(0)
+    d2_plain(1, -1, 3)
     for way, half in ((1, 0), (-1, 1)):
         arrive(("bzf", way), w_half(2, 0, half))
         w_out_half(2, half)
+    d2_plain(0, 1, 1)
+    w_in_forwards(1)
+    d2()
+    w_in_forwards(-1)
+    w_in_forwards(2)
     w_in_rest(1)
+    c1(0)
+    accumulate(1)
     w_in_rest(-1)
-    w_in_forwards(2)
+    accumulate(3)
+    c2(0)
     w_in_rest(2)
-
-    kept = count[0]
-    total[...] = jnp.zeros_like(total)
-
-    def accumulate(i, carry):
-        base = (i * 2 + c) * 4
-        picked = []
-        for q in range(4):
-            hid = jnp.where(base + q < kept, hid_ids[0, base + q], -1)
-            picked.append(feats[feat_ids[0, base + q]].reshape(256, 128))
-            block = weights[i, q]
-            for j in range(7):
-                spread[j * 128 : (j + 1) * 128, q * 128 : (q + 1) * 128] = jnp.where(
-                    hid == j, block, jnp.zeros_like(block)
-                )
-        total[...] += lax.dot_general(
-            jnp.concatenate(picked, axis=1), spread[...], (((1,), (1,)), ((), ())),
-            preferred_element_type=F32,
-        )
-        return carry
-
-    lax.fori_loop(0, 16, accumulate, 0)
+    accumulate(2)
+    c3(0)
 
     send("gh", total.at[pl.ds(pl.multiple_of((1 - c) * 128, 128), 128)], other, sib)
 
-    arrive(("d2", 0), u2.at[0])
-    arrive(("d2", 1), u2.at[1])
+    for half in (0, 1):
+        arrive(("dp", half), u2.at[half, piece(1 - half)])
+        arrive(("ds", half), u2.at[half, piece(half)])
     for q in range(4):
         mine = part[0, q] + u2[0, q].astype(F32) + u2[1, q].astype(F32)
         live = jnp.where(dp * 4 + q < kept, 1.0, 0.0)
@@ -303,13 +352,14 @@
 
     for copy in sent:
         copy.wait_send()
-    assert len(names) <= send_sems.shape[0]
+    assert len(names) == len(started) == len(arrived) <= send_sems.shape[0]
 
 
 def per_device(gate_in, up_in, cotangent, w_down, block_hidden, block_feat, kept_counts):
     vmem = pl.BlockSpec(memory_space=pltpu.VMEM)
+    hbm = pl.BlockSpec(memory_space=pl.ANY)
     smem = pl.BlockSpec(memory_space=pltpu.SMEM)
-    copies = 112
+    copies = 128
     return pl.pallas_call(
         kernel,
         out_shape=(
@@ -317,9 +367,12 @@
             jax.ShapeDtypeStruct(up_in.shape, BF16),
             jax.ShapeDtypeStruct(w_down.shape, BF16),
         ),
-        in_specs=[vmem, vmem, vmem, vmem, smem, smem, smem],
+        in_specs=[hbm, hbm, hbm, hbm, smem, smem, smem],
         out_specs=(vmem, vmem, vmem),
         scratch_shapes=[
+            pltpu.VMEM(gate_in.shape, BF16),
+            pltpu.VMEM(up_in.shape, BF16),
+            pltpu.VMEM(cotangent.shape, BF16),
             pltpu.VMEM((2, 16, 16, 16, 128), BF16),
             pltpu.VMEM((32, 16, 16, 128), BF16),
             pltpu.VMEM((2, 7, 128, 128), BF16),
@@ -339,9 +392,10 @@
             pltpu.VMEM((2, 4, 128, 128), BF16),
             pltpu.SemaphoreType.DMA((copies,)),
             pltpu.SemaphoreType.DMA((copies,)),
+            pltpu.SemaphoreType.DMA((4,)),
         ],
         compiler_params=pltpu.CompilerParams(
-            collective_id=0, has_side_effects=True, vmem_limit_bytes=48 * 2**20
+            collective_id=0, has_side_effects=True, vmem_limit_bytes=60 * 2**20
         ),
     )(gate_in, up_in, cotangent, w_down, block_hidden, block_feat, kept_counts)
 

time: 92.5 us -> 82 us (0.89)
  the two profiles are of different devices: /device:TPU:1 before, /device:TPU:65 now
where the time goes in v2:
time: 82 us; the launch traced here: 81.8 us
  Pallas kernels  77.2 us (94%)
  local copies, waits for them, and re-layouts  3.33 us (4%)
  between operations  1.3 us (2%)
    pallas_call x1, Pallas kernels, per_device(): pl.pallas_call(kernel, out_shape=(jax.ShapeDtypeStruct(gate_in.shape, BF1...  77.2 us
    unnamed x7, local copies, waits for them, and re-layouts  3.33 us

profile of v2, /device:TPU:65, one launch (start us, length us, event | category | flops | bytes accessed | tf_op | source)
XLA Modules:
  0.0 81.8 jit_solution(841080205820292803)
XLA Ops:
  1.3 77.2 %shard_map.94 = (bf16[128,896]{1,0:T(8,128)(2,1)}, bf16[128,896]{1,0:T(8,128)(2,1)}, bf16[1,4,128,128]{3,2,1,0:T(8,128)(2,1)}) custom-call(bf16[128,896]{1,0:T(8,128)(2,1)} %gate_hbm.1, bf16[128,896]{1,0:T(8,128)(2,1)} %up_hbm.1, bf16[8,4096]{1,0:T(8,128)(2,1)} %cot_hbm.1, bf16[1,4,128,128]{3,2,1,0:T(8,128)(2,1)} %w_hbm.1, s32[1,128]{1,0:T(1,128)} %hid_ids.1, ...), custom_call_target="tpu_custom_call" | custom-call | tf_op jit(solution)/shard_map/pallas_call | solution.py:363
  78.5 0.0 copy-start
  78.5 1.7 %copy.14 = bf16[128,896]{1,0:T(8,128)(2,1)} copy(bf16[128,896]{1,0:T(8,128)(2,1)} %get-tuple-element.6) | data formatting | bytes 458752
  80.1 0.0 copy-done
  80.2 0.0 copy-start.1
  80.2 0.7 copy.15
  80.8 0.3 copy-done.1
  81.1 0.7 copy.16
Async XLA Ops:
  78.5 1.7 %copy-start = (bf16[128,896]{1,0:T(8,128)(2,1)S(1)}, bf16[128,896]{1,0:T(8,128)(2,1)}, u32[]{:S(2)}) copy-start(bf16[128,896]{1,0:T(8,128)(2,1)} %get-tuple-element.7) | copy-start | bytes 688132
  80.2 1.0 %copy-start.1 = (bf16[1,4,128,128]{3,2,1,0:T(8,128)(2,1)S(1)}, bf16[1,4,128,128]{3,2,1,0:T(8,128)(2,1)}, u32[]{:S(2)}) copy-start(bf16[1,4,128,128]{3,2,1,0:T(8,128)(2,1)} %get-tuple-element.8) | copy-start | bytes 393220

commit v3 on v2

--- a/solution.py
+++ b/solution.py
@@ -8,11 +8,14 @@
 MESH = pl.DeviceIdType.MESH
 F32 = jnp.float32
 BF16 = jnp.bfloat16
+FORWARD = ((1, 0), (-1, 1))
+OTHER = ((1, 1), (-1, 0))
+DIRECT = (3,)
 
 
 def kernel(
     gate_hbm, up_hbm, cot_hbm, w_hbm, hid_ids, feat_ids, count,
-    gg, gu, gd,
+    grad, down,
     gate, up, cot, raw, feats, hid_t, weights, spread, total, other,
     prod, s1, r1, s2, r2, part, t1, u1, t2, u2,
     send_sems, recv_sems, load_sems,
@@ -31,7 +34,7 @@
     sib = dev(other_core=True)
     yd = {1: dev(dy=1), -1: dev(dy=3)}
     zd = {1: dev(dz=1), -1: dev(dz=3)}
-    xd = {1: dev(dx=1), -1: dev(dx=3)}
+    xd = {1: dev(dx=1), -1: dev(dx=3), 2: dev(dx=2)}
     ld = {k: dev(dl=k) for k in (1, 2, 3)}
 
     names = {}
@@ -109,11 +112,18 @@
         send(("ax", 1, k), own, own, xd[1])
         send(("ax", -1, k), own, own, xd[-1])
         send(("as", 0, k), own, own, sib)
-
-    def w_out(dz, order=((1, 0), (-1, 1), (1, 1), (-1, 0))):
-        for way, half in order:
-            block = w_half(dz, 0, half)
-            send(("by", way, dz, half), block, block, yd[way])
+        if k in DIRECT:
+            send(("ax", 2, k), own, own, xd[2])
+
+    def w_out_y(pieces):
+        for way, half in pieces:
+            block = w_half(0, 0, half)
+            send(("by", way, 0, half), block, block, yd[way])
+
+    def w_out_z(pieces):
+        for way, half in pieces:
+            block = w_half(0, 0, half)
+            send(("bz", way, half), block, block, zd[way])
 
     def w_out_half(dz, half):
         block = w_half(dz, 0, half)
@@ -123,54 +133,47 @@
     def w_in(way, dz, half):
         block = w_half(dz, -way % 4, half)
         arrive(("by", way, dz, half), block)
-        if (way, half) in ((1, 0), (-1, 1)):
+        if (way, half) in FORWARD:
             send(("bf", way, dz), block, block, yd[way])
 
-    def w_in_forwards(dz):
-        w_in(1, dz, 0)
-        w_in(-1, dz, 1)
-
-    def w_in_rest(dz):
-        w_in(1, dz, 1)
-        w_in(-1, dz, 0)
-        arrive(("bf", 1, dz), w_half(dz, 2, 0))
-        arrive(("bf", -1, dz), w_half(dz, 2, 1))
+    def w_in_far(dz, way):
+        arrive(("bf", way, dz), w_half(dz, 2, 0 if way == 1 else 1))
+
+    def wz_in(way, half):
+        block = w_half(-way, 0, half)
+        arrive(("bz", way, half), block)
+        if (way, half) in FORWARD:
+            send(("bzf", way), block, block, zd[way])
+
+    def wz_in_far(way):
+        arrive(("bzf", way), w_half(2, 0, 0 if way == 1 else 1))
 
     own = cot_block(0, 0)
     for k in (1, 2, 3):
         send(("al", k), own, own, ld[k])
     cot_out(0)
-    for way, half in ((1, 0), (-1, 1), (1, 1), (-1, 0)):
-        block = w_half(0, 0, half)
-        send(("bz", way, half), block, block, zd[way])
-    w_out(0)
-
     send("hid", hid_t.at[c], hid_t.at[c], sib)
 
     def cot_in_lo(k):
         arrive(("al", k), cot_block(0, k))
         cot_out(k)
 
-    def cot_in_x(k):
-        for way, half in ((1, 0), (-1, 1)):
-            arrive(("ax", way, k), cot_block(-way, k))
-            piece = cot_half(-way, k, half)
-            send(("af", way, k), piece, piece, xd[way])
-            block = cot_block(-way, k)
-            send(("as", -way, k), block, block, sib)
+    def cot_in_x(k, way):
+        block = cot_block(-way, k)
+        arrive(("ax", way, k), block)
+        if k not in DIRECT:
+            part_of = cot_half(-way, k, 0 if way == 1 else 1)
+            send(("af", way, k), part_of, part_of, xd[way])
+        send(("as", -way, k), block, block, sib)
 
     def cot_in_far(k):
-        arrive(("af", 1, k), cot_half(2, k, 0))
-        arrive(("af", -1, k), cot_half(2, k, 1))
         block = cot_block(2, k)
+        if k in DIRECT:
+            arrive(("ax", 2, k), block)
+        else:
+            arrive(("af", 1, k), cot_half(2, k, 0))
+            arrive(("af", -1, k), cot_half(2, k, 1))
         send(("as", 2, k), block, block, sib)
-
-    def wz_in(way, half):
-        block = w_half(-way, 0, half)
-        arrive(("bz", way, half), block)
-        if (way, half) in ((1, 0), (-1, 1)):
-            send(("bzf", way), block, block, zd[way])
-        w_out_half(-way, half)
 
     def repack(dx):
         def step(i, carry):
@@ -211,144 +214,193 @@
         for half, way in ((0, 1), (1, -1)):
             s1[dz, half] = prod[dz, 2, pair(half)].astype(BF16)
             send(("c1", dz, half), s1.at[dz, half], r1.at[dz, half], yd[way])
+
+    def cp(dz):
         for half, way, dy in ((0, 1, 1), (1, -1, 3)):
             rest = 1 - half
             s2[dz, half, pair(rest)] = prod[dz, dy, pair(rest)].astype(BF16)
             send(("cp", dz, half), s2.at[dz, half, piece(rest)], r2.at[dz, half, piece(rest)], yd[way])
 
-    def c2(dz):
-        for half, way, dy in ((0, 1, 1), (1, -1, 3)):
-            arrive(("c1", dz, half), r1.at[dz, half])
-            s2[dz, half, pair(half)] = (
-                prod[dz, dy, pair(half)] + r1[dz, half].astype(F32)
-            ).astype(BF16)
-            send(("cs", dz, half), s2.at[dz, half, piece(half)], r2.at[dz, half, piece(half)], yd[way])
-
-    def c3(dz):
-        for half in (0, 1):
-            arrive(("cp", dz, half), r2.at[dz, half, piece(1 - half)])
-        for half in (0, 1):
-            arrive(("cs", dz, half), r2.at[dz, half, piece(half)])
-        part[dz] = prod[dz, 0] + r2[dz, 0].astype(F32) + r2[dz, 1].astype(F32)
-
-    def d1():
-        for half, way in ((0, 1), (1, -1)):
-            t1[half] = part[2, pair(half)].astype(BF16)
-            send(("d1", half), t1.at[half], u1.at[half], zd[way])
-
-    def d2_plain(half, way, dz):
+    def c2(dz, half):
+        way, dy = ((1, 1), (-1, 3))[half]
+        arrive(("c1", dz, half), r1.at[dz, half])
+        s2[dz, half, pair(half)] = (prod[dz, dy, pair(half)] + r1[dz, half].astype(F32)).astype(BF16)
+        send(("cs", dz, half), s2.at[dz, half, piece(half)], r2.at[dz, half, piece(half)], yd[way])
+
+    def c3(dz, half):
+        other_half = 1 - half
+        arrive(("cp", dz, other_half), r2.at[dz, other_half, piece(half)])
+        arrive(("cs", dz, half), r2.at[dz, half, piece(half)])
+        rows = pair(half)
+        part[dz, rows] = prod[dz, 0, rows] + r2[dz, 0, rows].astype(F32) + r2[dz, 1, rows].astype(F32)
+
+    def d1(half):
+        t1[half] = part[2, pair(half)].astype(BF16)
+        send(("d1", half), t1.at[half], u1.at[half], zd[(1, -1)[half]])
+
+    def d2_plain(dz):
+        half, way = {1: (0, 1), 3: (1, -1)}[dz]
         rest = 1 - half
         t2[half, pair(rest)] = part[dz, pair(rest)].astype(BF16)
         send(("dp", half), t2.at[half, piece(rest)], u2.at[half, piece(rest)], zd[way])
 
-    def d2():
-        for half, way, dz in ((0, 1, 1), (1, -1, 3)):
-            arrive(("d1", half), u1.at[half])
-            t2[half, pair(half)] = (part[dz, pair(half)] + u1[half].astype(F32)).astype(BF16)
-            send(("ds", half), t2.at[half, piece(half)], u2.at[half, piece(half)], zd[way])
+    def d2(half):
+        way, dz = ((1, 1), (-1, 3))[half]
+        arrive(("d1", half), u1.at[half])
+        t2[half, pair(half)] = (part[dz, pair(half)] + u1[half].astype(F32)).astype(BF16)
+        send(("ds", half), t2.at[half, piece(half)], u2.at[half, piece(half)], zd[way])
 
     kept = count[0]
 
-    def accumulate(dz):
-        def place(dy, carry):
-            at = ((zh + dz) % 4) * 4 + (y + dy) % 4
-            base = (at * 2 + c) * 4
-            picked = []
-            for q in range(4):
-                hid = jnp.where(base + q < kept, hid_ids[0, base + q], -1)
-                picked.append(feats[feat_ids[0, base + q]].reshape(256, 128))
-                block = weights[at, q]
-                for j in range(7):
-                    spread[j * 128 : (j + 1) * 128, q * 128 : (q + 1) * 128] = jnp.where(
-                        hid == j, block, jnp.zeros_like(block)
-                    )
-            total[...] += lax.dot_general(
-                jnp.concatenate(picked, axis=1), spread[...], (((1,), (1,)), ((), ())),
-                preferred_element_type=F32,
-            )
-            return carry
-
-        lax.fori_loop(0, 4, place, 0)
+    def accumulate(dz, dy):
+        at = ((zh + dz) % 4) * 4 + (y + dy) % 4
+        base = (at * 2 + c) * 4
+        picked = []
+        for q in range(4):
+            hid = jnp.where(base + q < kept, hid_ids[0, base + q], -1)
+            picked.append(feats[feat_ids[0, base + q]].reshape(256, 128))
+            block = weights[at, q]
+            for j in range(7):
+                spread[j * 128 : (j + 1) * 128, q * 128 : (q + 1) * 128] = jnp.where(
+                    hid == j, block, jnp.zeros_like(block)
+                )
+        total[...] += lax.dot_general(
+            jnp.concatenate(picked, axis=1), spread[...], (((1,), (1,)), ((), ())),
+            preferred_element_type=F32,
+        )
+
+    def exchange():
+        send("gh", total.at[pl.ds(pl.multiple_of((1 - c) * 128, 128), 128)], other, sib)
+
+    def block_sums():
+        for half in (0, 1):
+            arrive(("dp", half), u2.at[half, piece(1 - half)])
+            arrive(("ds", half), u2.at[half, piece(half)])
+        for q in range(4):
+            live = jnp.where(dp * 4 + q < kept, 1.0, 0.0)
+            down[0, q] = (part[0, q] + u2[0, q].astype(F32) + u2[1, q].astype(F32)) * live
+
+    def finish():
+        arrive("gh", other)
+        grad[...] = total[pl.ds(pl.multiple_of(c * 128, 128), 128), :] + other[...]
 
     cot_in_lo(1)
+    w_out_y(FORWARD)
+    w_out_z(FORWARD)
+    w_out_y(OTHER)
+    cot_in_lo(2)
     cot_in_lo(3)
-    cot_in_x(1)
-    cot_in_lo(2)
-    cot_in_x(0)
-    cot_in_x(3)
-    cot_in_x(2)
+    cot_in_x(1, 1)
+    from_sib(0, (0, 1, 2, 3))
+    repack(0)
+    cot_in_x(1, -1)
     arrive("hid", hid_t.at[1 - c])
-    w_in_forwards(0)
+    w_in(1, 0, 0)
+    cot_in_x(0, 1)
+    cot_in_x(0, -1)
+    cot_in_x(2, -1)
+    cot_in_x(2, 1)
+    cot_in_x(3, 1)
+    w_in(1, 0, 1)
+    w_out_z(OTHER)
+    w_in(-1, 0, 1)
+    w_in(-1, 0, 0)
+    cot_in_x(3, -1)
+    cot_in_far(3)
+    wz_in(-1, 1)
+    w_out_half(1, 1)
+    wz_in(1, 0)
+    from_sib(1, (0, 1, 2, 3))
+    repack(1)
+    cot_in_far(1)
+    cot_in_far(0)
+    cot_in_far(2)
     from_sib(-1, (0, 1, 2, 3))
     repack(3)
-    wz_in(1, 0)
-    wz_in(-1, 1)
-    from_sib(0, (0, 1, 2, 3))
-    repack(0)
-    cot_in_far(1)
-    cot_in_far(3)
-    cot_in_far(2)
-    cot_in_far(0)
+    w_out_half(-1, 0)
     from_sib(2, (0, 1, 2, 3))
     repack(2)
-    from_sib(1, (0, 1, 2, 3))
-    repack(1)
-    w_in_rest(0)
+    w_in_far(0, -1)
     products(2)
     c1(2)
+    products(3)
     products(1)
+    c1(3)
+    cp(2)
     c1(1)
+    c2(2, 1)
+    c2(2, 0)
+    accumulate(0, 0)
+    cp(1)
+    c2(1, 1)
+    c2(1, 0)
+    wz_in(1, 1)
+    c2(3, 1)
+    c2(3, 0)
+    cp(3)
+    wz_in(-1, 0)
+    c3(2, 0)
+    d1(0)
+    c3(2, 1)
+    d1(1)
+    wz_in_far(1)
     products(0)
-    c2(2)
-    products(3)
-    c1(3)
-    c3(2)
-    d1()
-    c2(1)
-    c2(3)
-    wz_in(1, 1)
-    wz_in(-1, 0)
-    accumulate(0)
-    c3(3)
-    c3(1)
-    d2_plain(1, -1, 3)
-    for way, half in ((1, 0), (-1, 1)):
-        arrive(("bzf", way), w_half(2, 0, half))
-        w_out_half(2, half)
-    d2_plain(0, 1, 1)
-    w_in_forwards(1)
-    d2()
-    w_in_forwards(-1)
-    w_in_forwards(2)
-    w_in_rest(1)
+    w_in(-1, 1, 1)
+    w_in(1, 1, 1)
+    w_in(1, -1, 0)
+    w_out_half(-1, 1)
+    accumulate(1, 0)
+    accumulate(3, 0)
+    w_in(-1, -1, 0)
+    c3(1, 1)
+    w_out_half(2, 0)
+    wz_in_far(-1)
+    c3(3, 0)
+    w_out_half(2, 1)
+    d2_plain(1)
+    d2_plain(3)
+    c3(3, 1)
+    w_out_half(1, 0)
+    accumulate(0, 3)
+    w_in_far(0, 1)
+    w_in(1, -1, 1)
     c1(0)
-    accumulate(1)
-    w_in_rest(-1)
-    accumulate(3)
-    c2(0)
-    w_in_rest(2)
-    accumulate(2)
-    c3(0)
-
-    send("gh", total.at[pl.ds(pl.multiple_of((1 - c) * 128, 128), 128)], other, sib)
-
-    for half in (0, 1):
-        arrive(("dp", half), u2.at[half, piece(1 - half)])
-        arrive(("ds", half), u2.at[half, piece(half)])
-    for q in range(4):
-        mine = part[0, q] + u2[0, q].astype(F32) + u2[1, q].astype(F32)
-        live = jnp.where(dp * 4 + q < kept, 1.0, 0.0)
-        gd[0, q] = (mine * live).astype(BF16)
-
-    arrive("gh", other)
-    for j in range(7):
-        cols = slice(j * 128, (j + 1) * 128)
-        grad = total[pl.ds(pl.multiple_of(c * 128, 128), 128), cols] + other[:, cols]
-        g = gate[:, cols].astype(F32)
-        u = up[:, cols].astype(F32)
-        sigma = 1.0 / (1.0 + jnp.exp(-g))
-        gg[:, cols] = (grad * u * sigma * (1.0 + g * (1.0 - sigma))).astype(BF16)
-        gu[:, cols] = (grad * (g * sigma)).astype(BF16)
+    w_in(1, 2, 0)
+    accumulate(2, 0)
+    c3(1, 0)
+    d2(0)
+    d2(1)
+    accumulate(0, 2)
+    w_in(-1, -1, 1)
+    w_in(1, 1, 0)
+    w_in(-1, 2, 1)
+    accumulate(1, 3)
+    accumulate(3, 1)
+    w_in(-1, 1, 0)
+    accumulate(0, 1)
+    c2(0, 1)
+    accumulate(3, 3)
+    w_in_far(-1, 1)
+    w_in(1, 2, 1)
+    cp(0)
+    w_in(-1, 2, 0)
+    accumulate(2, 1)
+    w_in_far(1, -1)
+    accumulate(2, 3)
+    w_in_far(2, 1)
+    c2(0, 0)
+    accumulate(1, 1)
+    w_in_far(-1, -1)
+    w_in_far(2, -1)
+    accumulate(3, 2)
+    accumulate(2, 2)
+    w_in_far(1, 1)
+    accumulate(1, 2)
+    exchange()
+    c3(0, 1)
+    c3(0, 0)
+    block_sums()
+    finish()
 
     for copy in sent:
         copy.wait_send()
@@ -360,15 +412,14 @@
     hbm = pl.BlockSpec(memory_space=pl.ANY)
     smem = pl.BlockSpec(memory_space=pltpu.SMEM)
     copies = 128
-    return pl.pallas_call(
+    grad, down = pl.pallas_call(
         kernel,
         out_shape=(
-            jax.ShapeDtypeStruct(gate_in.shape, BF16),
-            jax.ShapeDtypeStruct(up_in.shape, BF16),
-            jax.ShapeDtypeStruct(w_down.shape, BF16),
+            jax.ShapeDtypeStruct(gate_in.shape, F32),
+            jax.ShapeDtypeStruct(w_down.shape, F32),
         ),
         in_specs=[hbm, hbm, hbm, hbm, smem, smem, smem],
-        out_specs=(vmem, vmem, vmem),
+        out_specs=(vmem, vmem),
         scratch_shapes=[
             pltpu.VMEM(gate_in.shape, BF16),
             pltpu.VMEM(up_in.shape, BF16),
@@ -398,6 +449,11 @@
             collective_id=0, has_side_effects=True, vmem_limit_bytes=60 * 2**20
         ),
     )(gate_in, up_in, cotangent, w_down, block_hidden, block_feat, kept_counts)
+    g, u = gate_in.astype(F32), up_in.astype(F32)
+    sigma = jax.nn.sigmoid(g)
+    grad_gate = (grad * u * sigma * (1.0 + g * (1.0 - sigma))).astype(BF16)
+    grad_up = (grad * (g * sigma)).astype(BF16)
+    return grad_gate, grad_up, down.astype(BF16)
 
 
 def solution(mesh):

time: 82 us -> 73.4 us (0.90)
  the two profiles are of different devices: /device:TPU:65 before, /device:TPU:1 now
where the time goes in v3:
time: 73.4 us; the launch traced here: 73.2 us
  Pallas kernels  69.1 us (94%)
  other arithmetic  2.73 us (4%)
  between operations  1.33 us (2%)
    pallas_call x1, Pallas kernels, per_device(): pl.pallas_call(kernel, out_shape=(jax.ShapeDtypeStruct(gate_in.shape, F32...  69.1 us
    convert_element_type x1, other arithmetic, per_device(): grad_up = (grad * (g * sigma)).astype(BF16)  2.06 us

profile of v3, /device:TPU:1, one launch (start us, length us, event | category | flops | bytes accessed | tf_op | source)
XLA Modules:
  0.0 73.2 jit_solution(5824566500387291468)
XLA Ops:
  1.3 0.0 copy-start
  1.3 0.0 copy-start.1
  1.3 69.1 %shard_map.94 = (f32[128,896]{1,0:T(8,128)}, f32[1,4,128,128]{3,2,1,0:T(8,128)}) custom-call(bf16[128,896]{1,0:T(8,128)(2,1)} %gate_hbm.1, bf16[128,896]{1,0:T(8,128)(2,1)} %up_hbm.1, bf16[8,4096]{1,0:T(8,128)(2,1)} %cot_hbm.1, bf16[1,4,128,128]{3,2,1,0:T(8,128)(2,1)} %w_hbm.1, s32[1,128]{1,0:T(1,128)} %hid_ids.1, s32[1,128]{1,0:T(1,128)} %feat_ids.1, ...), custom_call_target="tpu_custom_call" | custom-call | tf_op jit(solution)/shard_map/pallas_call | solution.py:415
  70.4 0.0 copy-done
  70.5 0.0 copy-done.1
  70.5 0.0 copy-start.2
  70.5 2.1 %fusion.7 = (bf16[128,896]{1,0:T(8,128)(2,1)}, bf16[128,896]{1,0:T(8,128)(2,1)}) fusion(f32[128,896]{1,0:T(8,128)} %get-tuple-element.5, bf16[128,896]{1,0:T(8,128)(2,1)S(1)} %copy-done, bf16[128,896]{1,0:T(8,128)(2,1)S(1)} %copy-done.1), kind=kLoop, calls=%fused_computation.10 | loop fusion | flops 1720320 | bytes 1376256 | tf_op jit(solution)/shard_map/convert_element_type | solution.py:455
  72.5 0.0 copy-done.2
  72.5 0.7 convert_element_type.19
Async XLA Ops:
  1.3 69.2 %copy-start = (bf16[128,896]{1,0:T(8,128)(2,1)S(1)}, bf16[128,896]{1,0:T(8,128)(2,1)}, u32[]{:S(2)}) copy-start(bf16[128,896]{1,0:T(8,128)(2,1)} %gate_hbm.1) | copy-start | bytes 688132
  1.3 69.2 %copy-start.1 = (bf16[128,896]{1,0:T(8,128)(2,1)S(1)}, bf16[128,896]{1,0:T(8,128)(2,1)}, u32[]{:S(2)}) copy-start(bf16[128,896]{1,0:T(8,128)(2,1)} %up_hbm.1) | copy-start | bytes 688132
  70.5 2.1 %copy-start.2 = (f32[1,4,128,128]{3,2,1,0:T(8,128)S(1)}, f32[1,4,128,128]{3,2,1,0:T(8,128)}, u32[]{:S(2)}) copy-start(f32[1,4,128,128]{3,2,1,0:T(8,128)} %get-tuple-element.6) | copy-start | bytes 786436

commit v4 on v3

--- a/solution.py
+++ b/solution.py
@@ -18,7 +18,7 @@
     grad, down,
     gate, up, cot, raw, feats, hid_t, weights, spread, total, other,
     prod, s1, r1, s2, r2, part, t1, u1, t2, u2,
-    send_sems, recv_sems, load_sems,
+    send_sems, recv_sems, load_sems, ready, z_ready,
 ):
     dp, tn = lax.axis_index("dp"), lax.axis_index("tensor")
     zh, y, c = dp // 8, (dp // 2) % 4, dp % 2
@@ -63,9 +63,19 @@
         ).wait_recv()
 
     barrier = pltpu.get_barrier_semaphore()
-    partners = [sib, *yd.values(), *zd.values(), *xd.values(), *ld.values()]
-    for partner in partners:
-        pl.semaphore_signal(barrier, inc=1, device_id=partner, device_id_type=MESH)
+    near = [*yd.values(), *xd.values(), *ld.values()]
+
+    def signal(sem, to):
+        pl.semaphore_signal(sem, inc=1, device_id=to, device_id_type=MESH)
+
+    @pl.when(c == 0)
+    def _():
+        for neighbour in near:
+            signal(barrier, neighbour)
+
+    @pl.when(c == 1)
+    def _():
+        signal(barrier, sib)
 
     loads = [
         pltpu.make_async_copy(src, dst, load_sems.at[n])
@@ -93,7 +103,29 @@
     total[...] = jnp.zeros_like(total)
     loads[3].wait()
 
-    pl.semaphore_wait(barrier, len(partners))
+    @pl.when(c == 0)
+    def _():
+        pl.semaphore_wait(barrier, len(near) + 1)
+        for neighbour in near:
+            signal(ready, neighbour)
+        pl.semaphore_wait(ready, len(near))
+        signal(ready, sib)
+
+    @pl.when(c == 1)
+    def _():
+        pl.semaphore_wait(ready, 1)
+        for partner in zd.values():
+            signal(barrier, partner)
+
+    def through_z():
+        @pl.when(c == 1)
+        def _():
+            pl.semaphore_wait(barrier, 2)
+            signal(z_ready, sib)
+
+        @pl.when(c == 0)
+        def _():
+            pl.semaphore_wait(z_ready, 1)
 
     def cot_block(dx, k):
         return raw.at[c, ((x + dx) % 4) * 4 + (zl - k + 4) % 4]
@@ -284,121 +316,122 @@
         arrive("gh", other)
         grad[...] = total[pl.ds(pl.multiple_of(c * 128, 128), 128), :] + other[...]
 
+    w_out_y(OTHER)
+    w_out_y(FORWARD)
+    cot_in_x(0, 1)
+    through_z()
+    w_out_z(FORWARD)
+    w_in(1, 0, 1)
+    cot_in_x(0, -1)
+    cot_in_lo(2)
     cot_in_lo(1)
-    w_out_y(FORWARD)
-    w_out_z(FORWARD)
-    w_out_y(OTHER)
-    cot_in_lo(2)
+    cot_in_far(0)
     cot_in_lo(3)
+    w_in(1, 0, 0)
     cot_in_x(1, 1)
+    cot_in_x(1, -1)
+    w_in(-1, 0, 1)
+    cot_in_x(2, 1)
+    w_out_z(OTHER)
+    cot_in_x(2, -1)
+    wz_in(-1, 1)
+    wz_in(1, 0)
+    cot_in_x(3, 1)
+    cot_in_x(3, -1)
     from_sib(0, (0, 1, 2, 3))
     repack(0)
-    cot_in_x(1, -1)
-    arrive("hid", hid_t.at[1 - c])
-    w_in(1, 0, 0)
-    cot_in_x(0, 1)
-    cot_in_x(0, -1)
-    cot_in_x(2, -1)
-    cot_in_x(2, 1)
-    cot_in_x(3, 1)
-    w_in(1, 0, 1)
-    w_out_z(OTHER)
-    w_in(-1, 0, 1)
-    w_in(-1, 0, 0)
-    cot_in_x(3, -1)
+    w_out_half(-1, 0)
+    w_out_half(1, 1)
     cot_in_far(3)
-    wz_in(-1, 1)
-    w_out_half(1, 1)
-    wz_in(1, 0)
+    cot_in_far(1)
+    cot_in_far(2)
     from_sib(1, (0, 1, 2, 3))
     repack(1)
-    cot_in_far(1)
-    cot_in_far(0)
-    cot_in_far(2)
+    w_in_far(0, 1)
+    arrive("hid", hid_t.at[1 - c])
     from_sib(-1, (0, 1, 2, 3))
     repack(3)
-    w_out_half(-1, 0)
     from_sib(2, (0, 1, 2, 3))
     repack(2)
-    w_in_far(0, -1)
     products(2)
     c1(2)
     products(3)
+    c1(3)
     products(1)
-    c1(3)
+    w_in(-1, -1, 0)
+    c1(1)
     cp(2)
-    c1(1)
+    c2(2, 0)
     c2(2, 1)
-    c2(2, 0)
-    accumulate(0, 0)
-    cp(1)
-    c2(1, 1)
-    c2(1, 0)
-    wz_in(1, 1)
-    c2(3, 1)
     c2(3, 0)
     cp(3)
-    wz_in(-1, 0)
+    cp(1)
+    w_in_far(0, -1)
+    w_in(1, 1, 1)
+    accumulate(0, 0)
+    c2(1, 1)
+    wz_in_far(1)
     c3(2, 0)
     d1(0)
+    w_in(-1, 0, 0)
+    wz_in(-1, 0)
     c3(2, 1)
     d1(1)
-    wz_in_far(1)
-    products(0)
-    w_in(-1, 1, 1)
-    w_in(1, 1, 1)
-    w_in(1, -1, 0)
+    wz_in(1, 1)
     w_out_half(-1, 1)
+    accumulate(0, 2)
+    wz_in_far(-1)
     accumulate(1, 0)
-    accumulate(3, 0)
-    w_in(-1, -1, 0)
+    c2(3, 1)
+    accumulate(2, 0)
+    accumulate(0, 1)
+    c2(1, 0)
+    accumulate(0, 3)
+    w_out_half(2, 0)
     c3(1, 1)
-    w_out_half(2, 0)
-    wz_in_far(-1)
-    c3(3, 0)
+    w_in(1, -1, 1)
     w_out_half(2, 1)
     d2_plain(1)
+    w_out_half(1, 0)
+    c3(3, 0)
     d2_plain(3)
     c3(3, 1)
-    w_out_half(1, 0)
-    accumulate(0, 3)
-    w_in_far(0, 1)
-    w_in(1, -1, 1)
+    w_in(1, 2, 0)
+    w_in(-1, -1, 1)
+    c3(1, 0)
+    products(0)
     c1(0)
-    w_in(1, 2, 0)
-    accumulate(2, 0)
-    c3(1, 0)
+    w_in(-1, 2, 0)
+    w_in(-1, 2, 1)
+    w_in(1, 2, 1)
     d2(0)
+    w_in(1, -1, 0)
+    w_in(-1, 1, 1)
+    w_in(-1, 1, 0)
+    w_in(1, 1, 0)
     d2(1)
-    accumulate(0, 2)
-    w_in(-1, -1, 1)
-    w_in(1, 1, 0)
-    w_in(-1, 2, 1)
-    accumulate(1, 3)
-    accumulate(3, 1)
-    w_in(-1, 1, 0)
-    accumulate(0, 1)
-    c2(0, 1)
-    accumulate(3, 3)
-    w_in_far(-1, 1)
-    w_in(1, 2, 1)
-    cp(0)
-    w_in(-1, 2, 0)
+    accumulate(3, 0)
     accumulate(2, 1)
-    w_in_far(1, -1)
-    accumulate(2, 3)
-    w_in_far(2, 1)
     c2(0, 0)
     accumulate(1, 1)
+    c2(0, 1)
+    cp(0)
     w_in_far(-1, -1)
+    accumulate(1, 3)
+    accumulate(3, 3)
+    accumulate(3, 1)
+    w_in_far(2, 1)
+    accumulate(2, 3)
     w_in_far(2, -1)
+    w_in_far(-1, 1)
+    w_in_far(1, -1)
     accumulate(3, 2)
-    accumulate(2, 2)
     w_in_far(1, 1)
     accumulate(1, 2)
+    accumulate(2, 2)
     exchange()
+    c3(0, 0)
     c3(0, 1)
-    c3(0, 0)
     block_sums()
     finish()
 
@@ -444,6 +477,8 @@
             pltpu.SemaphoreType.DMA((copies,)),
             pltpu.SemaphoreType.DMA((copies,)),
             pltpu.SemaphoreType.DMA((4,)),
+            pltpu.SemaphoreType.REGULAR,
+            pltpu.SemaphoreType.REGULAR,
         ],
         compiler_params=pltpu.CompilerParams(
             collective_id=0, has_side_effects=True, vmem_limit_bytes=60 * 2**20

time: 73.4 us -> 73 us (level)
  no operation moved by 1% of the time
where the time goes in v4:
time: 73 us; the launch traced here: 72.8 us
  Pallas kernels  68.7 us (94%)
  other arithmetic  2.73 us (4%)
  between operations  1.33 us (2%)
    pallas_call x1, Pallas kernels, per_device(): pl.pallas_call(kernel, out_shape=(jax.ShapeDtypeStruct(gate_in.shape, F32...  68.7 us
    convert_element_type x1, other arithmetic, per_device(): grad_up = (grad * (g * sigma)).astype(BF16)  2.06 us

profile of v4, /device:TPU:1, one launch (start us, length us, event | category | flops | bytes accessed | tf_op | source)
XLA Modules:
  0.0 72.8 jit_solution(7154520366982104182)
XLA Ops:
  1.3 0.0 copy-start
  1.3 0.0 copy-start.1
  1.3 68.7 %shard_map.94 = (f32[128,896]{1,0:T(8,128)}, f32[1,4,128,128]{3,2,1,0:T(8,128)}) custom-call(bf16[128,896]{1,0:T(8,128)(2,1)} %gate_hbm.1, bf16[128,896]{1,0:T(8,128)(2,1)} %up_hbm.1, bf16[8,4096]{1,0:T(8,128)(2,1)} %cot_hbm.1, bf16[1,4,128,128]{3,2,1,0:T(8,128)(2,1)} %w_hbm.1, s32[1,128]{1,0:T(1,128)} %hid_ids.1, s32[1,128]{1,0:T(1,128)} %feat_ids.1, ...), custom_call_target="tpu_custom_call" | custom-call | tf_op jit(solution)/shard_map/pallas_call | solution.py:448
  70.0 0.0 copy-done
  70.0 0.0 copy-done.1
  70.0 0.0 copy-start.2
  70.0 2.1 %fusion.7 = (bf16[128,896]{1,0:T(8,128)(2,1)}, bf16[128,896]{1,0:T(8,128)(2,1)}) fusion(f32[128,896]{1,0:T(8,128)} %get-tuple-element.5, bf16[128,896]{1,0:T(8,128)(2,1)S(1)} %copy-done, bf16[128,896]{1,0:T(8,128)(2,1)S(1)} %copy-done.1), kind=kLoop, calls=%fused_computation.10 | loop fusion | flops 1720320 | bytes 1376256 | tf_op jit(solution)/shard_map/convert_element_type | solution.py:490
  72.1 0.0 copy-done.2
  72.1 0.7 convert_element_type.19
Async XLA Ops:
  1.3 68.7 %copy-start = (bf16[128,896]{1,0:T(8,128)(2,1)S(1)}, bf16[128,896]{1,0:T(8,128)(2,1)}, u32[]{:S(2)}) copy-start(bf16[128,896]{1,0:T(8,128)(2,1)} %gate_hbm.1) | copy-start | bytes 688132
  1.3 68.7 %copy-start.1 = (bf16[128,896]{1,0:T(8,128)(2,1)S(1)}, bf16[128,896]{1,0:T(8,128)(2,1)}, u32[]{:S(2)}) copy-start(bf16[128,896]{1,0:T(8,128)(2,1)} %up_hbm.1) | copy-start | bytes 688132
  70.0 2.1 %copy-start.2 = (f32[1,4,128,128]{3,2,1,0:T(8,128)S(1)}, f32[1,4,128,128]{3,2,1,0:T(8,128)}, u32[]{:S(2)}) copy-start(f32[1,4,128,128]{3,2,1,0:T(8,128)} %get-tuple-element.6) | copy-start | bytes 786436
